TPU v7x, 32 devices: a whole 2x2x4 slice. The times are simulated.
32 devices in a mesh: samp: 8 (over z, y), var: 4 (over x, core).
Axes of the slice: x: 2, y: 2, z: 4, core: 2. Of those that a mesh axis runs over, the one named last changes fastest.
Arguments:
- genotypes: int32 [2048, 4096], P('samp', 'var'), may hold values from -1 to 2, as said below
- ancestry: float32 [16, 2048], P(None, 'samp'), may hold values from 0.05 to 4, as said below
- frequency: float32 [16, 4096], P(None, 'var'), may hold values from 0.05 to 0.95
Outputs:
- new_ancestry: float32 [16, 2048], P(None, 'samp')
- new_frequency: float32 [16, 4096], P(None, 'var')
Inputs may be any that keep to these rules, and one draw needn't show every extreme that they name: `genotypes`: A dosage of 0, 1 or 2 alternate alleles, or -1 for a missing genotype. `ancestry`: positive weights.
All inputs are finite; a program needn't handle non-finite values.
Results may differ from a plain program's by a relative error of at most 0.0003.
Values sent between devices are 32-bit elements; how exact they have to be, the bound alone decides.
A program may use at most 64 MiB of HBM per device.

v0:
```python
import jax
import jax.numpy as jnp
from jax import lax
from jax.sharding import PartitionSpec as P

ITERS = 4
HIGH = lax.Precision.HIGHEST


def contract(left, right, left_dim, right_dim):
    return lax.dot_general(
        left,
        right,
        (((left_dim,), (right_dim,)), ((), ())),
        precision=HIGH,
        preferred_element_type=jnp.float32,
    )


def shards(genotypes, ancestry, frequency):
    present = (genotypes >= 0).astype(jnp.float32)
    dosage = jnp.maximum(genotypes, 0).astype(jnp.float32)
    weight_ref = present * dosage
    weight_alt = present * (2.0 - dosage)
    fraction = ancestry / jnp.sum(ancestry, axis=0, keepdims=True)
    for sweep in range(ITERS):
        expected = contract(fraction, frequency, 0, 0)
        ratio_ref = weight_ref / expected
        ratio_alt = weight_alt / (1.0 - expected)
        partial_value = contract(frequency, ratio_ref, 1, 1) + contract(
            1.0 - frequency, ratio_alt, 1, 1
        )
        total = lax.psum(partial_value, "var")
        weighted = fraction * total
        fraction = weighted / jnp.sum(weighted, axis=0, keepdims=True)
        expected = contract(fraction, frequency, 0, 0)
        ratio_ref = weight_ref / expected
        ratio_alt = weight_alt / (1.0 - expected)
        term_ref = contract(fraction, ratio_ref, 1, 0)
        term_alt = contract(fraction, ratio_alt, 1, 0)
        sum_ref, sum_alt = lax.psum((term_ref, term_alt), "samp")
        upper = frequency * sum_ref
        lower = (1.0 - frequency) * sum_alt
        frequency = upper / (upper + lower)
    return (fraction, frequency)


def solution(mesh):
    return jax.shard_map(
        shards,
        mesh=mesh,
        in_specs=(P("samp", "var"), P(None, "samp"), P(None, "var")),
        out_specs=(P(None, "samp"), P(None, "var")),
        check_vma=False,
    )
```

profile of v0, /device:TPU:0, one launch (start us, length us, event | category | flops | bytes accessed | tf_op | source)
XLA Modules:
  0.0 370.3 jit_solution(9430064719370559565)
XLA Ops:
  7.2 0.0 copy-start.1
  7.2 0.0 copy-start.3
  7.2 0.0 all-reduce.15.cloned.1.call-start
  7.2 0.8 reduce_sum.45
  8.1 0.0 copy-start
  8.1 1.9 fusion.36
  10.0 1.1 convolution_bitcast_fusion
  11.1 1.1 convolution_add_fusion.3
  12.2 12.7 %psum.84 = f32[16,256]{1,0:T(8,128)S(1)} all-reduce(f32[16,256]{1,0:T(8,128)S(1)} %convolution_add_fusion.3), channel_id=1, replica_groups=mesh['samp'=8,'var'=4] {'var'}, use_global_device_ids=true, to_apply=%region_1.0 | all-reduce | flops 4096 | bytes 32768 | tf_op jit(solution)/shard_map/psum | solution.py:33
  24.9 1.0 fusion.52
  25.9 1.5 fusion.15
  27.5 1.5 fusion.12
  28.9 0.0 all-reduce.15.cloned.1.call-update
  29.0 0.0 all-reduce.13.cloned.1.call-start
  29.0 70.3 %all-reduce.15.cloned.1.call-done = (f32[16,1024]{1,0:T(8,128)}, f32[16,1024]{1,0:T(8,128)}) async-done(((f32[16,1024]{1,0:T(8,128)}, f32[16,1024]{1,0:T(8,128)}), (f32[16,1024]{1,0:T(8,128)}, f32[16,1024]{1,0:T(8,128)})) %all-reduce.15.cloned.1.call-update) | async-done | bytes 131088 | tf_op jit(solution)/shard_map/psum | solution.py:41
  99.3 0.9 add_divide_fusion.3
  100.2 1.0 fusion.53
  101.3 1.0 fusion.10
  102.3 1.1 convolution_add_fusion.2
  103.4 10.1 %psum.87 = f32[16,256]{1,0:T(8,128)S(1)} all-reduce(f32[16,256]{1,0:T(8,128)S(1)} %convolution_add_fusion.2), channel_id=1, replica_groups=mesh['samp'=8,'var'=4] {'var'}, use_global_device_ids=true, to_apply=%region_5.0 | all-reduce | flops 4096 | bytes 32768 | tf_op jit(solution)/shard_map/psum | solution.py:33
  113.5 1.0 fusion.48
  114.5 1.5 fusion.16
  116.1 1.5 fusion.8
  117.5 0.0 all-reduce.13.cloned.1.call-update
  117.6 0.2 all-reduce.11.cloned.1.call-start
  117.8 69.2 %all-reduce.13.cloned.1.call-done = (f32[16,1024]{1,0:T(8,128)}, f32[16,1024]{1,0:T(8,128)}) async-done(((f32[16,1024]{1,0:T(8,128)}, f32[16,1024]{1,0:T(8,128)}), (f32[16,1024]{1,0:T(8,128)}, f32[16,1024]{1,0:T(8,128)})) %all-reduce.13.cloned.1.call-update) | async-done | bytes 131088 | tf_op jit(solution)/shard_map/psum | solution.py:41
  187.0 0.9 add_divide_fusion.2
  187.8 1.0 fusion.47
  188.9 1.0 fusion.6
  189.9 1.1 convolution_add_fusion.1
  191.0 10.1 %psum.90 = f32[16,256]{1,0:T(8,128)S(1)} all-reduce(f32[16,256]{1,0:T(8,128)S(1)} %convolution_add_fusion.1), channel_id=1, replica_groups=mesh['samp'=8,'var'=4] {'var'}, use_global_device_ids=true, to_apply=%region_9.0 | all-reduce | flops 4096 | bytes 32768 | tf_op jit(solution)/shard_map/psum | solution.py:33
  201.1 1.0 fusion.54
  202.2 1.5 fusion.17
  203.7 1.5 fusion.4
  205.2 0.0 all-reduce.11.cloned.1.call-update
  205.2 0.0 all-reduce.9.cloned.1.call-start
  205.2 69.4 %all-reduce.11.cloned.1.call-done = (f32[16,1024]{1,0:T(8,128)}, f32[16,1024]{1,0:T(8,128)}) async-done(((f32[16,1024]{1,0:T(8,128)}, f32[16,1024]{1,0:T(8,128)}), (f32[16,1024]{1,0:T(8,128)}, f32[16,1024]{1,0:T(8,128)})) %all-reduce.11.cloned.1.call-update) | async-done | bytes 131088 | tf_op jit(solution)/shard_map/psum | solution.py:41
  274.6 0.9 add_divide_fusion.1
  275.5 1.0 fusion.55
  276.5 1.0 fusion.2
  277.6 1.1 convolution_add_fusion
  278.6 10.1 %psum.93 = f32[16,256]{1,0:T(8,128)S(1)} all-reduce(f32[16,256]{1,0:T(8,128)S(1)} %convolution_add_fusion), channel_id=1, replica_groups=mesh['samp'=8,'var'=4] {'var'}, use_global_device_ids=true, to_apply=%region_13.0 | all-reduce | flops 4096 | bytes 32768 | tf_op jit(solution)/shard_map/psum | solution.py:33
  288.8 1.0 fusion.56
  289.8 1.5 fusion.18
  291.4 1.5 fusion
  292.8 0.0 all-reduce.9.cloned.1.call-update
  292.9 69.4 %all-reduce.9.cloned.1.call-done = (f32[16,1024]{1,0:T(8,128)}, f32[16,1024]{1,0:T(8,128)}) async-done(((f32[16,1024]{1,0:T(8,128)}, f32[16,1024]{1,0:T(8,128)}), (f32[16,1024]{1,0:T(8,128)}, f32[16,1024]{1,0:T(8,128)})) %all-reduce.9.cloned.1.call-update) | async-done | bytes 131088 | tf_op jit(solution)/shard_map/psum | solution.py:41
  362.2 1.5 add_divide_fusion
  (12 shorter events, 0.1 us)
Async XLA Ops:
  7.2 0.9 copy-start.1
  7.2 2.8 copy-start.3
  7.2 92.1 %all-reduce.15.cloned.1.call-start = ((), (), s32[]{:S(2)}) async-start(), calls=%async_computation.3 | async-start | bytes 262144 | tf_op jit(solution)/shard_map/psum | solution.py:41
  8.1 2.0 copy-start
  29.0 158.0 %all-reduce.13.cloned.1.call-start = ((), (), s32[]{:S(2)}) async-start(), calls=%async_computation.2 | async-start | bytes 262144 | tf_op jit(solution)/shard_map/psum | solution.py:41
  117.6 157.1 %all-reduce.11.cloned.1.call-start = ((), (), s32[]{:S(2)}) async-start(), calls=%async_computation.1 | async-start | bytes 262144 | tf_op jit(solution)/shard_map/psum | solution.py:41
  205.2 157.1 %all-reduce.9.cloned.1.call-start = ((), (), s32[]{:S(2)}) async-start(), calls=%async_computation | async-start | bytes 262144 | tf_op jit(solution)/shard_map/psum | solution.py:41
  288.8 2.6 copy-start.2
Sparse Core Ops, SparseCore 0:
  29.1 70.2 all-reduce.14
  117.7 69.2 all-reduce.12
  205.3 69.2 all-reduce.10
  293.0 69.2 all-reduce.8
where the time goes:
time: 371 us; the launch traced here: 370 us
  waiting for transfers between devices  278 us (75%)
  blocking collectives  43 us (12%)
  matrix products  29.6 us (8%)
  between operations  13.9 us (4%)
  other arithmetic  5.13 us (1%)
    psum x4, waiting for transfers between devices, shards(): sum_ref, sum_alt = lax.psum((term_ref, term_alt), 'samp')  278 us
    psum x4, blocking collectives, shards(): total = lax.psum(partial_value, 'var')  43 us
    dot_general x24, matrix products, contract(): lax.dot_general(left, right, (((left_dim,), (right_dim,)), ((), ())), pre...  29.6 us
  transfers between devices with their start and end apart: 4, of which 4 were waited for; matrix products, arithmetic and copies ran while one was open for 0% of the time, Pallas kernels for 0%

commit v1 on v0

--- a/solution.py
+++ b/solution.py
@@ -30,7 +30,7 @@
         partial_value = contract(frequency, ratio_ref, 1, 1) + contract(
             1.0 - frequency, ratio_alt, 1, 1
         )
-        total = lax.psum(partial_value, "var")
+        total = jnp.sum(lax.all_gather(partial_value, "var"), axis=0)
         weighted = fraction * total
         fraction = weighted / jnp.sum(weighted, axis=0, keepdims=True)
         expected = contract(fraction, frequency, 0, 0)

time: 371 us -> 351 us (0.946)
  blocking collectives: 43 us -> 21.9 us
    psum x4 -> x0, blocking collectives: 43 us -> none  [shards(): total = lax.psum(partial_value, 'var')]
    all_gather x0 -> x4, blocking collectives: none -> 21.9 us  [shards(): total = jnp.sum(lax.all_gather(partial_value, 'var'), axis=0)]
where the time goes in v1:
time: 351 us; the launch traced here: 350 us
  waiting for transfers between devices  279 us (79%)
  matrix products  29.6 us (8%)
  blocking collectives  21.9 us (6%)
  between operations  13.9 us (4%)
  other arithmetic  5.16 us (1%)
    psum x4, waiting for transfers between devices, shards(): sum_ref, sum_alt = lax.psum((term_ref, term_alt), 'samp')  279 us
    dot_general x24, matrix products, contract(): lax.dot_general(left, right, (((left_dim,), (right_dim,)), ((), ())), pre...  29.6 us
    all_gather x4, blocking collectives, shards(): total = jnp.sum(lax.all_gather(partial_value, 'var'), axis=0)  21.9 us
  transfers between devices with their start and end apart: 4, of which 4 were waited for; matrix products, arithmetic and copies ran while one was open for 0% of the time, Pallas kernels for 0%

profile of v1, /device:TPU:0, one launch (start us, length us, event | category | flops | bytes accessed | tf_op | source)
XLA Modules:
  0.0 350.4 jit_solution(1947079237208516178)
XLA Ops:
  7.2 0.0 copy-start.1
  7.2 0.0 all-reduce.15.cloned.1.call-start
  7.2 0.8 reduce_sum.81
  8.1 0.0 copy-start
  8.1 1.9 fusion.36
  10.0 1.1 convolution_bitcast_fusion
  11.1 1.1 convolution_add_fusion.3
  12.2 6.2 %all-gather = f32[64,256]{1,0:T(8,128)S(1)} all-gather(f32[16,256]{1,0:T(8,128)S(1)} %convolution_add_fusion.3), channel_id=2, replica_groups=mesh['samp'=8,'var'=4] {'var'}, dimensions={0}, use_global_device_ids=true | all-gather | bytes 81920 | tf_op jit(solution)/shard_map/all_gather | solution.py:33
  18.4 1.0 fusion.52
  19.5 1.5 fusion.15
  21.0 1.5 fusion.12
  22.5 0.0 all-reduce.15.cloned.1.call-update
  22.5 0.0 all-reduce.13.cloned.1.call-start
  22.5 71.8 %all-reduce.15.cloned.1.call-done = (f32[16,1024]{1,0:T(8,128)}, f32[16,1024]{1,0:T(8,128)}) async-done(((f32[16,1024]{1,0:T(8,128)}, f32[16,1024]{1,0:T(8,128)}), (f32[16,1024]{1,0:T(8,128)}, f32[16,1024]{1,0:T(8,128)})) %all-reduce.15.cloned.1.call-update) | async-done | bytes 131088 | tf_op jit(solution)/shard_map/psum | solution.py:41
  94.3 0.9 add_divide_fusion.3
  95.2 1.0 fusion.53
  96.2 1.0 fusion.10
  97.2 1.1 convolution_add_fusion.2
  98.3 5.2 %all-gather.1 = f32[64,256]{1,0:T(8,128)S(1)} all-gather(f32[16,256]{1,0:T(8,128)S(1)} %convolution_add_fusion.2), channel_id=3, replica_groups=mesh['samp'=8,'var'=4] {'var'}, dimensions={0}, use_global_device_ids=true | all-gather | bytes 81920 | tf_op jit(solution)/shard_map/all_gather | solution.py:33
  103.6 1.0 fusion.48
  104.6 1.5 fusion.16
  106.2 1.5 fusion.8
  107.6 0.0 all-reduce.13.cloned.1.call-update
  107.7 0.2 all-reduce.11.cloned.1.call-start
  107.9 69.1 %all-reduce.13.cloned.1.call-done = (f32[16,1024]{1,0:T(8,128)}, f32[16,1024]{1,0:T(8,128)}) async-done(((f32[16,1024]{1,0:T(8,128)}, f32[16,1024]{1,0:T(8,128)}), (f32[16,1024]{1,0:T(8,128)}, f32[16,1024]{1,0:T(8,128)})) %all-reduce.13.cloned.1.call-update) | async-done | bytes 131088 | tf_op jit(solution)/shard_map/psum | solution.py:41
  177.0 0.9 add_divide_fusion.2
  177.8 1.0 fusion.47
  178.9 1.0 fusion.6
  179.9 1.1 convolution_add_fusion.1
  181.0 5.2 %all-gather.2 = f32[64,256]{1,0:T(8,128)S(1)} all-gather(f32[16,256]{1,0:T(8,128)S(1)} %convolution_add_fusion.1), channel_id=4, replica_groups=mesh['samp'=8,'var'=4] {'var'}, dimensions={0}, use_global_device_ids=true | all-gather | bytes 81920 | tf_op jit(solution)/shard_map/all_gather | solution.py:33
  186.3 1.0 fusion.54
  187.3 1.5 fusion.17
  188.9 1.5 fusion.4
  190.3 0.0 all-reduce.11.cloned.1.call-update
  190.3 0.0 all-reduce.9.cloned.1.call-start
  190.4 69.2 %all-reduce.11.cloned.1.call-done = (f32[16,1024]{1,0:T(8,128)}, f32[16,1024]{1,0:T(8,128)}) async-done(((f32[16,1024]{1,0:T(8,128)}, f32[16,1024]{1,0:T(8,128)}), (f32[16,1024]{1,0:T(8,128)}, f32[16,1024]{1,0:T(8,128)})) %all-reduce.11.cloned.1.call-update) | async-done | bytes 131088 | tf_op jit(solution)/shard_map/psum | solution.py:41
  259.6 0.9 add_divide_fusion.1
  260.5 1.0 fusion.55
  261.5 1.0 fusion.2
  262.6 1.1 convolution_add_fusion
  263.6 5.2 %all-gather.3 = f32[64,256]{1,0:T(8,128)S(1)} all-gather(f32[16,256]{1,0:T(8,128)S(1)} %convolution_add_fusion), channel_id=5, replica_groups=mesh['samp'=8,'var'=4] {'var'}, dimensions={0}, use_global_device_ids=true | all-gather | bytes 81920 | tf_op jit(solution)/shard_map/all_gather | solution.py:33
  268.9 0.0 copy-start.2
  268.9 1.0 fusion.56
  270.0 1.5 fusion.18
  271.5 1.5 fusion
  273.0 0.0 all-reduce.9.cloned.1.call-update
  273.0 69.3 %all-reduce.9.cloned.1.call-done = (f32[16,1024]{1,0:T(8,128)}, f32[16,1024]{1,0:T(8,128)}) async-done(((f32[16,1024]{1,0:T(8,128)}, f32[16,1024]{1,0:T(8,128)}), (f32[16,1024]{1,0:T(8,128)}, f32[16,1024]{1,0:T(8,128)})) %all-reduce.9.cloned.1.call-update) | async-done | bytes 131088 | tf_op jit(solution)/shard_map/psum | solution.py:41
  342.3 1.5 add_divide_fusion
  (16 shorter events, 0.2 us)
Async XLA Ops:
  7.2 0.9 copy-start.1
  7.2 2.8 copy-start.3
  7.2 87.1 %all-reduce.15.cloned.1.call-start = ((), (), s32[]{:S(2)}) async-start(), calls=%async_computation.3 | async-start | bytes 262144 | tf_op jit(solution)/shard_map/psum | solution.py:41
  8.1 2.0 copy-start
  22.5 154.5 %all-reduce.13.cloned.1.call-start = ((), (), s32[]{:S(2)}) async-start(), calls=%async_computation.2 | async-start | bytes 262144 | tf_op jit(solution)/shard_map/psum | solution.py:41
  107.7 152.0 %all-reduce.11.cloned.1.call-start = ((), (), s32[]{:S(2)}) async-start(), calls=%async_computation.1 | async-start | bytes 262144 | tf_op jit(solution)/shard_map/psum | solution.py:41
  190.3 152.0 %all-reduce.9.cloned.1.call-start = ((), (), s32[]{:S(2)}) async-start(), calls=%async_computation | async-start | bytes 262144 | tf_op jit(solution)/shard_map/psum | solution.py:41
  268.9 2.6 copy-start.2
Sparse Core Ops, SparseCore 0:
  22.6 71.6 all-reduce.14
  107.8 69.1 all-reduce.12
  190.5 69.1 all-reduce.10
  273.1 69.1 all-reduce.8
